TPU v7x, 256 devices: a whole 4x4x8 slice. The times are simulated.
256 devices in a mesh: blk: 64 (over z, y_hi, x), rep: 4 (over y_lo, core).
Axes of the slice: x: 4, y: 4 (y_hi: 2, y_lo: 2; y = y_hi * 2 + y_lo), z: 8, core: 2. Of those that a mesh axis runs over, the one named last changes fastest.
Arguments:
- features: bfloat16 [131072, 512], P('blk', 'rep'), may hold values from -6 to 6
- order: int32 [1024, 128], P('blk'), may hold values from 0 to 127, each once within a row
- columns: int32 [1024, 16], P('blk'), may hold values from 0 to 1023, as said below
- tiles: bfloat16 [1024, 16, 128, 128], P('blk'), may hold values from -0.125 to 0.125
- w_rel: bfloat16 [512, 512], P(None, 'rep'), may hold values from -0.25 to 0.25
- w_root: bfloat16 [512, 512], P(None, 'rep'), may hold values from -0.25 to 0.25
- upstream: bfloat16 [131072, 512], P('blk', 'rep'), may hold values from -6 to 6
Outputs:
- hidden: bfloat16 [131072, 512], P('blk', 'rep')
- grad_features: bfloat16 [131072, 512], P('blk', 'rep')
- grad_rel: float32 [512, 512], P(None, 'rep')
- grad_root: float32 [512, 512], P(None, 'rep')
Inputs may be any that keep to these rules, and one draw needn't show every extreme that they name: `order`: each row holds every number below 128 once. `columns`: blocks form groups of 16 consecutive blocks on a closed loop of 1024 / 16 groups; a block-row's 16 column blocks are distinct, include its own block, and lie in groups at most 3 steps from its own group along the loop; every block-row has one column block exactly 3 groups ahead and one exactly 3 groups behind.
All inputs are finite; a program needn't handle non-finite values.
Results may differ from a plain program's by a relative error of at most 0.015.
Values may be sent and summed in bfloat16 or wider, within the bound.
A program may use at most 128 MiB of HBM per device.

v0:
```python
import jax
import jax.numpy as jnp
from jax import lax
from jax.sharding import PartitionSpec as P

REACH = 3


def passed_along(value, axis, steps):
    count = lax.axis_size(axis)
    pairs = [(source, (source + steps) % count) for source in range(count)]
    return lax.ppermute(value, axis, pairs)


def activate(values):
    return jax.nn.gelu(values, approximate=True)


def relay_fetch(source, offset):
    return passed_along(source, "blk", offset)


def relay_push(source, offset):
    return passed_along(source.astype(jnp.bfloat16), "blk", offset).astype(source.dtype)


def on_device(features, order, columns, tiles, w_rel, w_root, upstream):
    blocks = order.shape[0]
    block_len = order.shape[1]
    per_row = columns.shape[1]
    panel_width = features.shape[1]
    row_count = blocks * block_len
    span_len = 2 * REACH + 1
    groups_total = lax.axis_size("blk")
    own_group = lax.axis_index("blk")
    rep_index = lax.axis_index("rep")
    ordered = jnp.take_along_axis(
        features.reshape(blocks, block_len, panel_width), order[:, :, None], axis=1
    )
    ordered_rows = ordered.reshape(row_count, panel_width)
    offset_ids = (columns // blocks - own_group + REACH) % groups_total
    slot_ids = offset_ids * blocks + columns % blocks
    ahead_list = []
    behind_list = []
    ahead_copy = ordered_rows
    behind_copy = ordered_rows
    for hop_index in range(REACH):
        ahead_copy = relay_fetch(ahead_copy, -1)
        behind_copy = relay_fetch(behind_copy, 1)
        ahead_list.append(ahead_copy)
        behind_list.append(behind_copy)
    window_list = behind_list[::-1] + [ordered_rows] + ahead_list
    window = jnp.stack(window_list).reshape(span_len * blocks, block_len, panel_width)
    picked = window[slot_ids]
    aggregated = jnp.einsum("bkij,bkjf->bif", tiles, picked, preferred_element_type=jnp.float32)
    aggregated = aggregated.astype(jnp.bfloat16).reshape(row_count, panel_width)
    agg_full, ordered_full = (
        lax.all_gather(aggregated, "rep", axis=1, tiled=True),
        lax.all_gather(ordered_rows, "rep", axis=1, tiled=True),
    )
    preact = jnp.dot(agg_full, w_rel, preferred_element_type=jnp.float32) + jnp.dot(
        ordered_full, w_root, preferred_element_type=jnp.float32
    )
    activated, pull_back = jax.vjp(activate, preact)
    grad_pre = pull_back(upstream.astype(jnp.float32))[0].astype(jnp.bfloat16)
    grad_rel, grad_root = lax.psum(
        (
            jnp.dot(agg_full.T, grad_pre, preferred_element_type=jnp.float32),
            jnp.dot(ordered_full.T, grad_pre, preferred_element_type=jnp.float32),
        ),
        "blk",
    )
    contract_last = (((1,), (1,)), ((), ()))
    pre_full, rel_full, root_full = (
        lax.all_gather(grad_pre, "rep", axis=1, tiled=True),
        lax.all_gather(w_rel, "rep", axis=1, tiled=True),
        lax.all_gather(w_root, "rep", axis=1, tiled=True),
    )
    rel_rows = lax.dynamic_slice_in_dim(rel_full, rep_index * panel_width, panel_width, 0)
    root_rows = lax.dynamic_slice_in_dim(root_full, rep_index * panel_width, panel_width, 0)
    grad_agg_cols = lax.dot_general(
        rel_rows, pre_full, contract_last, preferred_element_type=jnp.float32
    )
    root_cols = lax.dot_general(
        root_rows, pre_full, contract_last, preferred_element_type=jnp.float32
    )
    grad_agg = grad_agg_cols.astype(jnp.bfloat16).reshape(panel_width, blocks, block_len)
    contrib = jnp.einsum("bkji,fbj->bkif", tiles, grad_agg, preferred_element_type=jnp.float32)
    target_sums = jax.ops.segment_sum(
        contrib.reshape(blocks * per_row, block_len, panel_width),
        slot_ids.reshape(-1),
        num_segments=span_len * blocks,
    )
    target_sums = target_sums.reshape(span_len, row_count, panel_width)
    ahead_carry = target_sums[2 * REACH]
    behind_carry = target_sums[0]
    collected = target_sums[REACH]
    for hop_index in range(1, REACH + 1):
        ahead_recv = relay_push(ahead_carry, 1)
        behind_recv = relay_push(behind_carry, -1)
        if hop_index < REACH:
            ahead_carry = ahead_recv + target_sums[2 * REACH - hop_index]
            behind_carry = behind_recv + target_sums[hop_index]
        else:
            collected = collected + ahead_recv + behind_recv
    grad_ordered = (
        (collected + root_cols.T).astype(jnp.bfloat16).reshape(blocks, block_len, panel_width)
    )
    inverse = jnp.argsort(order, axis=1)
    grad_features = jnp.take_along_axis(grad_ordered, inverse[:, :, None], axis=1).reshape(
        row_count, panel_width
    )
    return (activated.astype(jnp.bfloat16), grad_features, grad_rel, grad_root)


def solution(mesh):
    in_specs = (
        P("blk", "rep"),
        P("blk", None),
        P("blk", None),
        P("blk", None, None, None),
        P(None, "rep"),
        P(None, "rep"),
        P("blk", "rep"),
    )
    out_specs = (P("blk", "rep"), P("blk", "rep"), P(None, "rep"), P(None, "rep"))
    return jax.shard_map(
        on_device, mesh=mesh, in_specs=in_specs, out_specs=out_specs, check_vma=False
    )
```

profile of v0, /device:TPU:2, one launch (start us, length us, event | category | flops | bytes accessed | tf_op | source)
XLA Modules:
  0.0 1045.1 jit_solution(7362988144043318957)
XLA Ops:
  9.5 11.1 %gather_fusion.1 = bf16[2048,128]{1,0:T(8,128)(2,1)S(1)} fusion(bf16[16,128,128]{2,1,0:T(8,128)(2,1)S(1)} %bitcast.98, s32[2048]{0:T(1024)S(1)} %or_bitcast_fusion.1), kind=kCustom, calls=%fused_computation.clone | custom fusion | bytes 1064960 | tf_op jit(solution)/shard_map/jit(take_along_axis)/gather | solution.py:37
  21.0 1.6 collective-permute-start
  22.6 0.9 collective-permute-start.3
  23.4 11.3 %collective-permute-done = bf16[2048,128]{1,0:T(8,128)(2,1)S(1)} collective-permute-done((bf16[2048,128]{1,0:T(8,128)(2,1)S(1)}, bf16[2048,128]{1,0:T(8,128)(2,1)S(1)}, u32[]{:S(2)}, u32[]{:S(2)}) %collective-permute-start) | collective-permute-done | bytes 524320 | tf_op jit(solution)/shard_map/ppermute | solution.py:12
  34.7 1.5 collective-permute-start.1
  36.2 8.0 collective-permute-start.4
  44.2 11.4 %collective-permute-done.1 = bf16[2048,128]{1,0:T(8,128)(2,1)S(1)} collective-permute-done((bf16[2048,128]{1,0:T(8,128)(2,1)S(1)}, bf16[2048,128]{1,0:T(8,128)(2,1)S(1)}, u32[]{:S(2)}, u32[]{:S(2)}) %collective-permute-start.1) | collective-permute-done | bytes 524320 | tf_op jit(solution)/shard_map/ppermute | solution.py:12
  55.7 7.5 collective-permute-start.5
  63.3 10.2 collective-permute-done.2
  73.5 0.9 bitcast_dynamic-update-slice_fusion.6
  74.4 0.8 bitcast_dynamic-update-slice_fusion.5
  75.2 0.8 bitcast_dynamic-update-slice_fusion.4
  76.0 0.9 bitcast_dynamic-update-slice_fusion.3
  76.8 0.8 bitcast_dynamic-update-slice_fusion.2
  78.5 0.8 bitcast_dynamic-update-slice_fusion
  79.3 10.7 %gather_fusion = bf16[256,128,128]{2,1,0:T(8,128)(2,1)} fusion(bf16[112,128,128]{2,1,0:T(8,128)(2,1)} %bitcast.13, s32[1024]{0:T(1024)S(1)} %pad_clamp_fusion), kind=kCustom, calls=%fused_computation.2 | custom fusion | bytes 16778240 | tf_op jit(solution)/shard_map/gather | solution.py:54
  90.0 8.9 fusion
  100.7 30.7 %all-gather.4.cloned.1.call-done = bf16[2048,512]{1,0:T(8,128)(2,1)} async-done(((bf16[2048,128]{1,0:T(8,128)(2,1)}), bf16[2048,512]{1,0:T(8,128)(2,1)}) %all-gather.4.cloned.1.call-update) | async-done | bytes 2097168 | tf_op jit(solution)/shard_map/all_gather | solution.py:58
  131.3 2.3 fusion.35
  133.6 32.6 %all-gather.6.cloned.1.call-done = bf16[2048,512]{1,0:T(8,128)(2,1)} async-done(((bf16[2048,128]{1,0:T(8,128)(2,1)}), bf16[2048,512]{1,0:T(8,128)(2,1)}) %all-gather.6.cloned.1.call-update) | async-done | bytes 2097168 | tf_op jit(solution)/shard_map/all_gather | solution.py:59
  166.2 3.6 fusion.4
  170.0 7.7 all_gather.17
  177.7 7.1 all_gather.19
  185.5 17.0 %all-gather.8.cloned.1.call-done = bf16[2048,512]{1,0:T(8,128)(2,1)} async-done(((bf16[2048,128]{1,0:T(8,128)(2,1)}), bf16[2048,512]{1,0:T(8,128)(2,1)}) %all-gather.8.cloned.1.call-update) | async-done | bytes 2097168 | tf_op jit(solution)/shard_map/all_gather | solution.py:75
  202.5 2.4 fusion.1
  205.0 11.5 %fusion.19 = f32[16,128,16,128]{3,1,2,0:T(8,128)} fusion(bf16[16,16,128,128]{3,2,1,0:T(8,128)(2,1)} %param.12, bf16[128,16,128,1]{2,1,0,3:T(8,128)(2,1)S(1)} %bitcast.106), kind=kOutput, calls=%fused_computation.36 | convolution fusion | flops 1073741824 | bytes 25690112 | tf_op jit(solution)/shard_map/bkji,fbj->bkif/dot_general | solution.py:88
  216.5 17.4 %copy.13 = f32[256,128,128]{2,1,0:T(8,128)} copy(f32[256,128,128]{1,2,0:T(8,128)} %bitcast.99) | data formatting | bytes 33554432 | tf_op jit(solution)/shard_map/reshape | solution.py:90
  233.9 3.8 broadcast_in_dim.20
  237.7 52.2 %scatter_fusion = f32[112,128,128]{2,1,0:T(8,128)} fusion(f32[112,128,128]{2,1,0:T(8,128)} %broadcast_in_dim.20, s32[256]{0:T(256)S(1)} %reshape.80, f32[256,128,128]{2,1,0:T(8,128)} %copy.13), kind=kCustom, calls=%fused_computation.3 | custom fusion | flops 4194304 | bytes 50332672 | tf_op jit(solution)/shard_map/scatter-add | solution.py:89
  289.9 4.1 convert.4
  294.1 1.5 collective-permute-start.6
  296.3 1.6 fusion.33
  297.9 10.5 %collective-permute-done.6 = bf16[2048,128]{1,0:T(8,128)(2,1)S(1)} collective-permute-done((bf16[2048,128]{1,0:T(8,128)(2,1)S(1)}, bf16[2048,128]{1,0:T(8,128)(2,1)S(1)}, u32[]{:S(2)}, u32[]{:S(2)}) %collective-permute-start.6) | collective-permute-done | bytes 524320 | tf_op jit(solution)/shard_map/ppermute | solution.py:12
  308.5 1.4 collective-permute-start.7
  310.3 6.1 collective-permute-start.10
  316.4 1.5 fusion.36
  317.8 10.4 collective-permute-done.7
  328.2 0.9 fusion.14
  329.1 0.9 fusion.12
  330.1 7.5 collective-permute-start.11
  337.5 1.4 fusion.37
  339.7 8.4 collective-permute-done.8
  348.3 1.8 fusion.18
  350.1 11.1 %gather_fusion.2 = bf16[2048,128]{1,0:T(8,128)(2,1)S(1)} fusion(bf16[16,128,128]{2,1,0:T(8,128)(2,1)S(1)} %bitcast.100, s32[2048]{0:T(1024)S(1)} %or_bitcast_fusion), kind=kCustom, calls=%fused_computation.1.clone | custom fusion | bytes 1064960 | tf_op jit(solution)/shard_map/jit(take_along_axis)/gather | solution.py:110
  361.2 1.1 broadcast_select_fusion
  362.4 672.3 %all-reduce.3.cloned.1.call-done = (f32[512,128]{1,0:T(8,128)}, f32[512,128]{1,0:T(8,128)}) async-done(((f32[512,128]{1,0:T(8,128)}, f32[512,128]{1,0:T(8,128)}), (f32[512,128]{1,0:T(8,128)}, f32[512,128]{1,0:T(8,128)})) %all-reduce.3.cloned.1.call-update) | async-done | bytes 524304 | tf_op jit(solution)/shard_map/psum | solution.py:66
  1034.6 1.7 copy.30
  1036.3 1.7 copy.31
  (62 shorter events, 7.6 us)
Async XLA Ops:
  8.0 1.5 copy-start
  8.0 47.6 %copy-start.11 = (s32[16,16]{1,0:T(8,128)S(1)}, s32[16,16]{1,0:T(8,128)}, u32[]{:S(2)}) copy-start(s32[16,16]{1,0:T(8,128)} %param.11) | copy-start | bytes 3076
  8.0 123.3 %all-gather.4.cloned.1.call-start = ((), (), s32[]{:S(2)}) async-start(), calls=%async_computation | async-start | bytes 2621440 | tf_op jit(solution)/shard_map/all_gather | solution.py:58
  21.0 58.3 %copy-start.5 = (bf16[16,128,128]{2,1,0:T(8,128)(2,1)}, bf16[16,128,128]{2,1,0:T(8,128)(2,1)S(1)}, u32[]{:S(2)}) copy-start(bf16[16,128,128]{2,1,0:T(8,128)(2,1)S(1)} %broadcast_select_fusion.1) | copy-start | bytes 1572868
  21.0 13.7 %collective-permute-start = (bf16[2048,128]{1,0:T(8,128)(2,1)S(1)}, bf16[2048,128]{1,0:T(8,128)(2,1)S(1)}, u32[]{:S(2)}, u32[]{:S(2)}) collective-permute-start(bf16[2048,128]{1,0:T(8,128)(2,1)S(1)} %bitcast.102), channel_id=1, source_target_pairs={{0,4},{4,8},{8,12},{12,16},{16,20},{20,24},{24,28},{28,32},{32,36}... | collective-permute-start | bytes 1572872 | tf_op jit(solution)/shard_map/ppermute | solution.py:12
  22.6 13.7 %collective-permute-start.3 = (bf16[2048,128]{1,0:T(8,128)(2,1)S(1)}, bf16[2048,128]{1,0:T(8,128)(2,1)S(1)}, u32[]{:S(2)}, u32[]{:S(2)}) collective-permute-start(bf16[2048,128]{1,0:T(8,128)(2,1)S(1)} %bitcast.103), channel_id=1, source_target_pairs={{0,252},{4,0},{8,4},{12,8},{16,12},{20,16},{24,20},{28,24},{32,28}... | collective-permute-start | bytes 1572872 | tf_op jit(solution)/shard_map/ppermute | solution.py:12
  34.7 20.8 %collective-permute-start.1 = (bf16[2048,128]{1,0:T(8,128)(2,1)S(1)}, bf16[2048,128]{1,0:T(8,128)(2,1)S(1)}, u32[]{:S(2)}, u32[]{:S(2)}) collective-permute-start(bf16[2048,128]{1,0:T(8,128)(2,1)S(1)} %collective-permute-done), channel_id=1, source_target_pairs={{0,4},{4,8},{8,12},{12,16},{16,20},{20,24},{24,28},{28,32},{32,36}... | collective-permute-start | bytes 1572872 | tf_op jit(solution)/shard_map/ppermute | solution.py:12
  36.2 19.5 %collective-permute-start.4 = (bf16[2048,128]{1,0:T(8,128)(2,1)S(1)}, bf16[2048,128]{1,0:T(8,128)(2,1)S(1)}, u32[]{:S(2)}, u32[]{:S(2)}) collective-permute-start(bf16[2048,128]{1,0:T(8,128)(2,1)S(1)} %collective-permute-done.3), channel_id=1, source_target_pairs={{0,252},{4,0},{8,4},{12,8},{16,12},{20,16},{24,20},{28,24},{32,28}... | collective-permute-start | bytes 1572872 | tf_op jit(solution)/shard_map/ppermute | solution.py:12
  55.6 17.9 %collective-permute-start.2 = (bf16[2048,128]{1,0:T(8,128)(2,1)S(1)}, bf16[2048,128]{1,0:T(8,128)(2,1)S(1)}, u32[]{:S(2)}, u32[]{:S(2)}) collective-permute-start(bf16[2048,128]{1,0:T(8,128)(2,1)S(1)} %collective-permute-done.1), channel_id=1, source_target_pairs={{0,4},{4,8},{8,12},{12,16},{16,20},{20,24},{24,28},{28,32},{32,36}... | collective-permute-start | bytes 1572872 | tf_op jit(solution)/shard_map/ppermute | solution.py:12
  55.7 22.8 %collective-permute-start.5 = (bf16[2048,128]{1,0:T(8,128)(2,1)S(1)}, bf16[2048,128]{1,0:T(8,128)(2,1)S(1)}, u32[]{:S(2)}, u32[]{:S(2)}) collective-permute-start(bf16[2048,128]{1,0:T(8,128)(2,1)S(1)} %collective-permute-done.4), channel_id=1, source_target_pairs={{0,252},{4,0},{8,4},{12,8},{16,12},{20,16},{24,20},{28,24},{32,28}... | collective-permute-start | bytes 1572872 | tf_op jit(solution)/shard_map/ppermute | solution.py:12
  90.0 41.3 %copy-start.8 = (bf16[512,128]{1,0:T(8,128)(2,1)S(1)}, bf16[512,128]{1,0:T(8,128)(2,1)}, u32[]{:S(2)}) copy-start(bf16[512,128]{1,0:T(8,128)(2,1)} %param.13) | copy-start | bytes 393220
  99.0 67.2 %copy-start.9 = (bf16[512,128]{1,0:T(8,128)(2,1)S(1)}, bf16[512,128]{1,0:T(8,128)(2,1)}, u32[]{:S(2)}) copy-start(bf16[512,128]{1,0:T(8,128)(2,1)} %param.14) | copy-start | bytes 393220
  99.0 67.2 %copy-start.12 = (bf16[2048,128]{1,0:T(8,128)(2,1)S(1)}, bf16[2048,128]{1,0:T(8,128)(2,1)}, u32[]{:S(2)}) copy-start(bf16[2048,128]{1,0:T(8,128)(2,1)} %param.15) | copy-start | bytes 1572868
  99.0 67.2 %all-gather.6.cloned.1.call-start = ((), (), s32[]{:S(2)}) async-start(), calls=%async_computation.1 | async-start | bytes 2621440 | tf_op jit(solution)/shard_map/all_gather | solution.py:59
  99.8 85.0 %sort.19.cloned.1.call-start = ((), (), s32[]{:S(2)}) async-start(), calls=%async_computation.4 | async-start | bytes 49184 | tf_op jit(solution)/shard_map/jit(argsort)/sort | solution.py:109
  100.4 102.1 %all-gather.8.cloned.1.call-start = ((), (), s32[]{:S(2)}) async-start(), calls=%async_computation.2 | async-start | bytes 2621440 | tf_op jit(solution)/shard_map/all_gather | solution.py:75
  169.9 864.8 %all-reduce.3.cloned.1.call-start = ((), (), s32[]{:S(2)}) async-start(), calls=%async_computation.3 | async-start | bytes 1048576 | tf_op jit(solution)/shard_map/psum | solution.py:66
  289.9 5.6 copy-start.10
  289.9 6.4 copy-start.2
  294.1 14.3 %collective-permute-start.6 = (bf16[2048,128]{1,0:T(8,128)(2,1)S(1)}, bf16[2048,128]{1,0:T(8,128)(2,1)S(1)}, u32[]{:S(2)}, u32[]{:S(2)}) collective-permute-start(bf16[2048,128]{1,0:T(8,128)(2,1)S(1)} %bitcast.112), channel_id=1, source_target_pairs={{0,4},{4,8},{8,12},{12,16},{16,20},{20,24},{24,28},{28,32},{32,36}... | collective-permute-start | bytes 1572872 | tf_op jit(solution)/shard_map/ppermute | solution.py:12
  295.6 14.6 %collective-permute-start.9 = (bf16[2048,128]{1,0:T(8,128)(2,1)S(1)}, bf16[2048,128]{1,0:T(8,128)(2,1)S(1)}, u32[]{:S(2)}, u32[]{:S(2)}) collective-permute-start(bf16[2048,128]{1,0:T(8,128)(2,1)S(1)} %bitcast.111), channel_id=1, source_target_pairs={{0,252},{4,0},{8,4},{12,8},{16,12},{20,16},{24,20},{28,24},{32,28}... | collective-permute-start | bytes 1572872 | tf_op jit(solution)/shard_map/ppermute | solution.py:12
  297.9 18.5 %copy-start.3 = (bf16[2048,512]{1,0:T(8,128)(2,1)S(1)}, bf16[2048,512]{1,0:T(8,128)(2,1)}, u32[]{:S(2)}) copy-start(bf16[2048,512]{1,0:T(8,128)(2,1)} %all-gather.4.cloned.1.call-done) | copy-start | bytes 6291460
  297.9 18.5 %copy-start.6 = (bf16[2048,128]{1,0:T(8,128)(2,1)S(1)}, bf16[2048,128]{1,0:T(8,128)(2,1)}, u32[]{:S(2)}) copy-start(bf16[2048,128]{1,0:T(8,128)(2,1)} %get-tuple-element.18) | copy-start | bytes 1572868
  308.5 19.7 %collective-permute-start.7 = (bf16[2048,128]{1,0:T(8,128)(2,1)S(1)}, bf16[2048,128]{1,0:T(8,128)(2,1)S(1)}, u32[]{:S(2)}, u32[]{:S(2)}) collective-permute-start(bf16[2048,128]{1,0:T(8,128)(2,1)S(1)} %fusion.15), channel_id=1, source_target_pairs={{0,4},{4,8},{8,12},{12,16},{16,20},{20,24},{24,28},{28,32},{32,36}... | collective-permute-start | bytes 1572872 | tf_op jit(solution)/shard_map/ppermute | solution.py:12
  310.3 27.2 %copy-start.7 = (bf16[2048,512]{1,0:T(8,128)(2,1)S(1)}, bf16[2048,512]{1,0:T(8,128)(2,1)}, u32[]{:S(2)}) copy-start(bf16[2048,512]{1,0:T(8,128)(2,1)} %all-gather.6.cloned.1.call-done) | copy-start | bytes 6291460
  310.3 18.8 %collective-permute-start.10 = (bf16[2048,128]{1,0:T(8,128)(2,1)S(1)}, bf16[2048,128]{1,0:T(8,128)(2,1)S(1)}, u32[]{:S(2)}, u32[]{:S(2)}) collective-permute-start(bf16[2048,128]{1,0:T(8,128)(2,1)S(1)} %fusion.13), channel_id=1, source_target_pairs={{0,252},{4,0},{8,4},{12,8},{16,12},{20,16},{24,20},{28,24},{32,28}... | collective-permute-start | bytes 1572872 | tf_op jit(solution)/shard_map/ppermute | solution.py:12
  328.2 10.8 %copy-start.4 = (bf16[2048,512]{1,0:T(8,128)(2,1)S(1)}, bf16[2048,512]{1,0:T(8,128)(2,1)}, u32[]{:S(2)}) copy-start(bf16[2048,512]{1,0:T(8,128)(2,1)} %all-gather.8.cloned.1.call-done) | copy-start | bytes 6291460
  329.1 19.0 %collective-permute-start.8 = (bf16[2048,128]{1,0:T(8,128)(2,1)}, bf16[2048,128]{1,0:T(8,128)(2,1)}, u32[]{:S(2)}, u32[]{:S(2)}) collective-permute-start(bf16[2048,128]{1,0:T(8,128)(2,1)} %fusion.14), channel_id=1, source_target_pairs={{0,4},{4,8},{8,12},{12,16},{16,20},{20,24},{24,28},{28,32},{32,36}... | collective-permute-start | bytes 1572872 | tf_op jit(solution)/shard_map/ppermute | solution.py:12
  330.1 18.3 %collective-permute-start.11 = (bf16[2048,128]{1,0:T(8,128)(2,1)}, bf16[2048,128]{1,0:T(8,128)(2,1)}, u32[]{:S(2)}, u32[]{:S(2)}) collective-permute-start(bf16[2048,128]{1,0:T(8,128)(2,1)} %fusion.12), channel_id=1, source_target_pairs={{0,252},{4,0},{8,4},{12,8},{16,12},{20,16},{24,20},{28,24},{32,28}... | collective-permute-start | bytes 1572872 | tf_op jit(solution)/shard_map/ppermute | solution.py:12
  350.1 687.9 %copy-start.1 = (bf16[2048,128]{1,0:T(8,128)(2,1)S(1)}, bf16[2048,128]{1,0:T(8,128)(2,1)}, u32[]{:S(2)}) copy-start(bf16[2048,128]{1,0:T(8,128)(2,1)} %param.9) | copy-start | bytes 1572868
Sparse Core Ops, SparseCore 0:
  99.1 32.1 all-gather.3
  133.7 32.4 all-gather.5
  170.0 32.4 all-gather.7
  339.1 695.4 all-reduce.2
Sparse Core Ops, SparseCore 1:
  103.0 2.2 sort.21.cloned.1.call-done
  (1 shorter events, 0.0 us)
where the time goes:
time: 1050 us
  waiting for transfers between devices  816 us (78%)
  local copies, waits for them, and re-layouts  66 us (6%)
  other arithmetic  63.8 us (6%)
  starting transfers between devices  37 us (4%)
  matrix products  32.3 us (3%)
  between operations  15.4 us (1%)
  blocking collectives  14.8 us (1%)
    psum x1, waiting for transfers between devices, on_device(): lax.psum((jnp.dot(agg_full.T, grad_pre, preferred_element_type=jnp.float3...  672 us
    ppermute x12, waiting for transfers between devices, passed_along(): return lax.ppermute(value, axis, pairs)  62.6 us
    scatter-add x1, other arithmetic, on_device(): jax.ops.segment_sum(contrib.reshape(blocks * per_row, block_len, panel_wi...  52.2 us
    ppermute x12, starting transfers between devices, passed_along(): return lax.ppermute(value, axis, pairs)  36.6 us
    all_gather x1, waiting for transfers between devices, on_device(): lax.all_gather(ordered_rows, 'rep', axis=1, tiled=True)  32.6 us
    all_gather x1, waiting for transfers between devices, on_device(): lax.all_gather(aggregated, 'rep', axis=1, tiled=True)  30.7 us
  transfers between devices with their start and end apart: 16, of which 12 were waited for; matrix products, arithmetic and copies ran while one was open for 3% of the time, Pallas kernels for 0%

commit v1 on v0

v1 whole, which is shorter than its diff:
```python
import jax
import jax.numpy as jnp
from jax import lax
from jax.experimental import pallas as pl
from jax.experimental.pallas import tpu as pltpu
from jax.sharding import PartitionSpec as P

MESH = pl.DeviceIdType.MESH
REACH = 3
SPAN = 2 * REACH + 1
ROW = 4
HALO_CHUNKS = 8
MID_CHUNKS = 8
BACK_CHUNKS = 8
BF = jnp.bfloat16
F32 = jnp.float32
NT = (((1,), (1,)), ((), ()))
TN = (((0,), (0,)), ((), ()))
MIB = 2**20


class Place:
    def __init__(self, groups):
        blk = lax.axis_index("blk")
        rep = lax.axis_index("rep")
        self.groups = groups
        self.rows = groups // ROW
        self.blk, self.rep = blk, rep
        x = lax.rem(blk, ROW)
        self.x = x
        self.row = lax.div(blk, ROW)
        half, odd = lax.div(x, 2), lax.rem(x, 2)
        self.n1 = 3 - x
        self.n2 = x + 1 - 2 * odd
        self.diag = lax.rem(x + 2, 4)
        self.step_p = 1 - 2 * half
        self.step_q = 1 - 2 * odd
        self.slot_n1 = REACH + self.n1 - x
        self.slot_n2 = REACH + self.n2 - x
        self.slot_diag = REACH + self.diag - x
        self.slot_p = REACH + self.n1 - x - ROW * self.step_p
        self.slot_q = REACH + self.n2 - x - ROW * self.step_q
        self.slot_post = 1 + 4 * half
        self.core = lax.rem(rep, 2)
        self.low = lax.div(rep, 2)
        self.rep_sib = 2 * self.low + 1 - self.core
        self.rep_y = 2 * (1 - self.low) + self.core
        self.rep_far = 2 * (1 - self.low) + 1 - self.core

    def at_x(self, x):
        return (self.row * ROW + x, self.rep)

    def at_row(self, row):
        return (row * ROW + self.x, self.rep)

    def row_by(self, step):
        return self.at_row(lax.rem(self.row + step + self.rows, self.rows))

    def at_rep(self, rep):
        return (self.blk, rep)


def greet(partners):
    barrier = pltpu.get_barrier_semaphore()
    for who in partners:
        pl.semaphore_signal(barrier, inc=1, device_id=who, device_id_type=MESH)
    pl.semaphore_wait(barrier, len(partners))


def remote(src, dst, send, recv, who):
    return pltpu.make_async_remote_copy(
        src_ref=src, dst_ref=dst, send_sem=send, recv_sem=recv, device_id=who, device_id_type=MESH
    )


def onehot(order_ref, b):
    length = order_ref.shape[1]
    node = lax.broadcasted_iota(jnp.int32, (length, length), 0)
    return (node == order_ref[pl.ds(b, 1), :]).astype(F32).astype(BF)


def slot_of(col, place, blocks):
    group = lax.div(col, blocks)
    offset = lax.rem(group - place.blk + REACH + place.groups, place.groups)
    return lax.min(offset, SPAN - 1) * blocks + lax.rem(col, blocks)


def forward_kernel(
    groups,
    cols, feat, order, tiles, w_rel, w_root, upstream,
    hidden, back_agg, back_root, wgrad,
    win, tbuf, agg, slab, keep, s1, r1, s2, r2, pre,
    tile_sem, hs, hr, ws, wr, ms, mr,
):
    me = Place(groups)
    blocks, bl, width = feat.shape
    per_row = cols.shape[1]
    own = REACH * blocks
    nc = HALO_CHUNKS
    hb = blocks // nc
    nm = MID_CHUNKS
    mb = blocks // nm
    mrows = mb * bl

    tile_copy = pltpu.make_async_copy(tiles, tbuf, tile_sem)
    tile_copy.start()
    sib, far_y, far = me.at_rep(me.rep_sib), me.at_rep(me.rep_y), me.at_rep(me.rep_far)
    greet([me.at_x(me.n1), me.at_x(me.n2), me.row_by(1), me.row_by(-1), sib, far_y, far])

    def halo(kind, c):
        src_slot, dst_slot, who = [
            (REACH, REACH + me.x - me.n1, me.at_x(me.n1)),
            (REACH, REACH + me.x - me.n2, me.at_x(me.n2)),
            (me.slot_n2, REACH + me.n2 - me.n1, me.at_x(me.n1)),
            (me.slot_n1, me.slot_p, me.row_by(me.step_p)),
            (me.slot_n2, me.slot_q, me.row_by(me.step_q)),
            (me.slot_p, me.slot_post, me.at_x(me.n2)),
        ][kind]
        return remote(
            win.at[pl.ds(src_slot * blocks + c * hb, hb)],
            win.at[pl.ds(dst_slot * blocks + c * hb, hb)],
            hs.at[kind, c], hr.at[kind, c], who,
        )

    @pl.loop(0, nc)
    def _(c):
        for i in range(hb):
            b = c * hb + i
            win[own + b] = lax.dot_general(
                onehot(order, b), feat[b], TN, preferred_element_type=F32
            ).astype(BF)
        halo(0, c).start()
        halo(1, c).start()

    def weight(i, j):
        who = (me.rep_sib, me.rep_y, me.rep_far)[i]
        src = (w_rel, w_root)[j]
        return remote(
            src.at[pl.ds(who * width, width)], slab.at[me.rep, pl.ds(j * width, width)],
            ws.at[i, j], wr.at[i, j], me.at_rep(who),
        )

    for i in range(3):
        for j in range(2):
            weight(i, j).start()
    for j, src in enumerate((w_rel, w_root)):
        slab[me.rep, j * width : (j + 1) * width] = src[pl.ds(me.rep * width, width), :]

    @pl.loop(0, nc + 2)
    def _(s):
        @pl.when(s < nc)
        def _():
            halo(0, s).wait_recv()
            halo(1, s).wait_recv()
            halo(2, s).start()
            halo(3, s).start()
            halo(4, s).start()

        @pl.when(s >= 2)
        def _():
            halo(3, s - 2).wait_recv()
            halo(5, s - 2).start()

    @pl.loop(0, nc)
    def _(c):
        for kind in (2, 4, 5):
            halo(kind, c).wait_recv()

    for i in range(3):
        for j in range(2):
            weight(i, j).wait_recv()
    tile_copy.wait()

    panel_sib = [2 * (1 - me.low) + 1 - me.core, 2 * me.low + 1 - me.core]
    panel_mine = [me.rep_y, me.rep]

    def rows(c):
        return pl.ds(c * mb, mb)

    def mid(kind, c):
        src, dst, who = [
            (s1.at[c], r1.at[c], sib),
            (s2.at[c], r2.at[c], far_y),
            (pre.at[me.rep, rows(c)], pre.at[me.rep, rows(c)], far_y),
            (pre.at[me.rep, rows(c)], pre.at[me.rep, rows(c)], sib),
            (pre.at[me.rep_y, rows(c)], pre.at[me.rep_y, rows(c)], sib),
        ][kind]
        return remote(src, dst, ms.at[kind, c], mr.at[kind, c], who)

    def both(c):
        return jnp.concatenate(
            [
                agg[rows(c)].reshape(mrows, width),
                win[pl.ds(own + c * mb, mb)].reshape(mrows, width),
            ],
            axis=1,
        )

    @pl.loop(0, nm + 4)
    def _(s):
        @pl.when(s < nm)
        def _():
            for i in range(mb):
                b = s * mb + i
                left = jnp.concatenate([tbuf[b, k] for k in range(per_row)], axis=1)
                right = jnp.concatenate(
                    [win[slot_of(cols[b, k], me, blocks)] for k in range(per_row)], axis=0
                )
                agg[b] = jnp.dot(left, right, preferred_element_type=F32).astype(BF)
            x = both(s)
            for i in range(2):
                part = jnp.dot(x, slab[panel_sib[i]], preferred_element_type=F32)
                s1[s, i] = part.astype(BF)
            mid(0, s).start()
            for i in range(2):
                keep[s, i] = jnp.dot(x, slab[panel_mine[i]], preferred_element_type=F32)

        @pl.when((s >= 1) & (s < nm + 1))
        def _():
            c = s - 1
            mid(0, c).wait_recv()
            s2[c] = (keep[c, 0] + r1[c, 0].astype(F32)).astype(BF)
            mid(1, c).start()

        @pl.when((s >= 2) & (s < nm + 2))
        def _():
            c = s - 2
            mid(1, c).wait_recv()
            v = keep[c, 1] + r1[c, 1].astype(F32) + r2[c].astype(F32)
            sq = v * v
            t = jnp.tanh(0.7978845608 * (v + 0.044715 * (sq * v)))
            up = upstream[rows(c)].reshape(mrows, width).astype(F32)
            hidden[rows(c)] = (0.5 * v * (1.0 + t)).astype(BF).reshape(mb, bl, width)
            slope = 0.5 * (1.0 + t) + 0.5 * v * (1.0 - t * t) * (
                0.7978845608 * (1.0 + 0.134145 * sq)
            )
            pre[me.rep, rows(c)] = (up * slope).astype(BF).reshape(mb, bl, width)
            mid(2, c).start()
            mid(3, c).start()

        @pl.when((s >= 3) & (s < nm + 3))
        def _():
            mid(2, s - 3).wait_recv()
            mid(4, s - 3).start()

        @pl.when(s >= 4)
        def _():
            c = s - 4
            mid(3, c).wait_recv()
            mid(4, c).wait_recv()
            x = both(c)
            gathered = jnp.concatenate(
                [pre[p, rows(c)].reshape(mrows, width) for p in range(4)], axis=1
            )
            slabs = jnp.concatenate([slab[p] for p in range(4)], axis=1)
            back = lax.dot_general(slabs, gathered, NT, preferred_element_type=F32)
            for i in range(mb):
                cut = back[:, i * bl : (i + 1) * bl]
                back_agg[c * mb + i] = cut[:width].astype(BF)
                back_root[c * mb + i] = cut[width:]
            grads = lax.dot_general(x, gathered, TN, preferred_element_type=F32)

            @pl.when(c == 0)
            def _():
                for p in range(4):
                    wgrad[p] = grads[:, p * width : (p + 1) * width]

            @pl.when(c > 0)
            def _():
                for p in range(4):
                    wgrad[p] += grads[:, p * width : (p + 1) * width]

    @pl.loop(0, nc)
    def _(c):
        for kind in range(6):
            halo(kind, c).wait_send()

    @pl.loop(0, nm)
    def _(c):
        for kind in range(5):
            mid(kind, c).wait_send()

    for i in range(3):
        for j in range(2):
            weight(i, j).wait_send()


def push_kernel(groups, cols, tiles, back_agg, sums, own_sums, acc):
    me = Place(groups)
    b = pl.program_id(0)
    steps, per_row = cols.shape
    blocks = steps

    @pl.when(b == 0)
    def _():
        acc[...] = jnp.zeros_like(acc)

    right = jnp.concatenate([tiles[0, k] for k in range(per_row)], axis=1)
    res = jnp.dot(back_agg[0], right, preferred_element_type=F32)
    bl = tiles.shape[-1]
    for k in range(per_row):
        acc[slot_of(cols[b, k], me, blocks)] += res[:, k * bl : (k + 1) * bl]

    @pl.when(b == steps - 1)
    def _():
        @pl.loop(0, acc.shape[0])
        def _(s):
            sums[s] = acc[s].astype(BF)

        @pl.loop(0, blocks)
        def _(s):
            own_sums[s] = acc[REACH * blocks + s]


def backward_kernel(
    groups,
    sums, own_sums, back_root, order, wgrad,
    grad_feat, grad_rel, grad_root,
    land, out, wsend, a0, a1, a2, a3, a4, piece, done,
    hs, hr, e0s, e0r, e1s, e1r, e2s, e2r, e3s, e3r, e4s, e4r,
):
    me = Place(groups)
    blocks, bl = order.shape
    width = own_sums.shape[1]
    nc = BACK_CHUNKS
    hb = blocks // nc
    rows = me.rows
    x_others = [me.n1, me.n2, me.diag]
    rep_others = [me.rep_sib, me.rep_y, me.rep_far]
    greet(
        [me.at_x(x) for x in x_others]
        + [me.at_rep(r) for r in rep_others]
        + [me.row_by(d) for d in range(1, rows)]
    )

    POST, DIAG, Q, PP, N2, N1 = range(6)

    def part(ref, slot, c):
        return ref.at[pl.ds(slot * blocks + c * hb, hb)]

    def halo(kind, c):
        src, who = [
            (part(sums, me.slot_post, c), me.at_x(me.n2)),
            (part(sums, me.slot_diag, c), me.at_x(me.n1)),
            (part(sums, me.slot_q, c), me.row_by(-me.step_q)),
            (part(out, 0, c), me.row_by(-me.step_p)),
            (part(out, 1, c), me.at_x(me.n2)),
            (part(out, 2, c), me.at_x(me.n1)),
        ][kind]
        return remote(src, part(land, kind, c), hs.at[kind, c], hr.at[kind, c], who)

    def got(kind, b):
        return land[kind * blocks + b].astype(F32)

    def local(slot, b):
        return sums[slot * blocks + b].astype(F32)

    def share(i):
        who = rep_others[i]
        return remote(wsend.at[who], a0.at[me.rep], e0s.at[i], e0r.at[i], me.at_rep(who))

    def along_x(i):
        who = x_others[i]
        return remote(a0.at[who], a1.at[i], e1s.at[i], e1r.at[i], me.at_x(who))

    def scatter_rows(d):
        who = lax.rem(me.row + d, rows)
        return remote(piece.at[who], a2.at[d], e2s.at[d], e2r.at[d], me.at_row(who))

    def gather_rows(d):
        who = lax.rem(me.row + d, rows)
        return remote(done, a3.at[me.row], e3s.at[d], e3r.at[d], me.at_row(who))

    def gather_x(i):
        return remote(a3, a4.at[me.x], e4s.at[i], e4r.at[i], me.at_x(x_others[i]))

    for p in range(4):
        wsend[p] = wgrad[p].astype(BF)
    for i in range(3):
        share(i).start()
    a0[me.rep] = wsend[me.rep]

    @pl.loop(0, nc)
    def _(c):
        halo(POST, c).start()
        halo(DIAG, c).start()
        halo(Q, c).start()

    @pl.loop(0, nc + 6)
    def _(s):
        @pl.when(s < nc)
        def _():
            c = s
            halo(POST, c).wait_recv()
            for i in range(hb):
                b = c * hb + i
                out[b] = (local(me.slot_p, b) + got(POST, b)).astype(BF)
            halo(PP, c).start()

        @pl.when((s >= 2) & (s < nc + 2))
        def _():
            c = s - 2
            halo(DIAG, c).wait_recv()
            halo(Q, c).wait_recv()
            for i in range(hb):
                b = c * hb + i
                out[blocks + b] = (local(me.slot_n2, b) + got(DIAG, b) + got(Q, b)).astype(BF)
            halo(N2, c).start()

        @pl.when((s >= 3) & (s < nc + 3))
        def _():
            c = s - 3
            halo(PP, c).wait_recv()
            for i in range(hb):
                b = c * hb + i
                out[2 * blocks + b] = (local(me.slot_n1, b) + got(PP, b)).astype(BF)
            halo(N1, c).start()

        @pl.when(s == 2)
        def _():
            for i in range(3):
                share(i).wait_recv()
            for i in range(3):
                along_x(i).start()

        @pl.when(s == 6)
        def _():
            for i in range(3):
                along_x(i).wait_recv()
            total = a0[me.x].astype(F32)
            for i in range(3):
                total += a1[i].astype(F32)
            piece[...] = total.reshape(piece.shape)
            for d in range(1, rows):
                scatter_rows(d).start()

        @pl.when(s == 8)
        def _():
            for d in range(1, rows):
                scatter_rows(d).wait_recv()
            total = piece[me.row]
            for d in range(1, rows):
                total += a2[d]
            done[...] = total
            a3[me.row] = total
            for d in range(1, rows):
                gather_rows(d).start()

        @pl.when(s == 10)
        def _():
            for d in range(1, rows):
                gather_rows(d).wait_recv()
            for i in range(3):
                gather_x(i).start()
            a4[me.x] = a3[...]

        @pl.when(s >= 6)
        def _():
            c = s - 6
            halo(N2, c).wait_recv()
            halo(N1, c).wait_recv()
            for i in range(hb):
                b = c * hb + i
                total = own_sums[b] + back_root[b] + got(N1, b) + got(N2, b)
                grad_feat[b] = lax.dot_general(
                    onehot(order, b), total.astype(BF), NT, preferred_element_type=F32
                ).astype(BF)

    for i in range(3):
        gather_x(i).wait_recv()
    for p in range(4):
        both = a4[p].reshape(2 * width, width)
        grad_rel[p * width : (p + 1) * width, :] = both[:width]
        grad_root[p * width : (p + 1) * width, :] = both[width:]

    @pl.loop(0, nc)
    def _(c):
        for kind in range(6):
            halo(kind, c).wait_send()

    for i in range(3):
        share(i).wait_send()
        along_x(i).wait_send()
        gather_x(i).wait_send()
    for d in range(1, rows):
        scatter_rows(d).wait_send()
        gather_rows(d).wait_send()


def on_device(features, order, columns, tiles, w_rel, w_root, upstream):
    groups = lax.axis_size("blk")
    blocks, bl = order.shape
    width = features.shape[1]
    rows = groups // ROW
    vmem = pl.BlockSpec(memory_space=pltpu.VMEM)
    smem = pl.BlockSpec(memory_space=pltpu.SMEM)
    anywhere = pl.BlockSpec(memory_space=pl.ANY)
    dma = pltpu.SemaphoreType.DMA
    cube = (blocks, bl, width)
    mrows = blocks // MID_CHUNKS * bl

    def shape(dims, dtype):
        return jax.ShapeDtypeStruct(dims, dtype)

    hidden, back_agg, back_root, wgrad = pl.pallas_call(
        lambda *refs: forward_kernel(groups, *refs),
        out_shape=(
            shape(cube, BF),
            shape((blocks, width, bl), BF),
            shape((blocks, width, bl), F32),
            shape((4, 2 * width, width), F32),
        ),
        in_specs=[smem, vmem, vmem, anywhere, vmem, vmem, vmem],
        out_specs=(vmem,) * 4,
        scratch_shapes=[
            pltpu.VMEM((SPAN * blocks, bl, width), BF),
            pltpu.VMEM(tiles.shape, BF),
            pltpu.VMEM(cube, BF),
            pltpu.VMEM((4, 2 * width, width), BF),
            pltpu.VMEM((MID_CHUNKS, 2, mrows, width), F32),
            pltpu.VMEM((MID_CHUNKS, 2, mrows, width), BF),
            pltpu.VMEM((MID_CHUNKS, 2, mrows, width), BF),
            pltpu.VMEM((MID_CHUNKS, mrows, width), BF),
            pltpu.VMEM((MID_CHUNKS, mrows, width), BF),
            pltpu.VMEM((4,) + cube, BF),
            dma(()),
            dma((6, HALO_CHUNKS)),
            dma((6, HALO_CHUNKS)),
            dma((3, 2)),
            dma((3, 2)),
            dma((5, MID_CHUNKS)),
            dma((5, MID_CHUNKS)),
        ],
        compiler_params=pltpu.CompilerParams(
            collective_id=0, has_side_effects=True, vmem_limit_bytes=56 * MIB
        ),
        name="forward",
    )(columns, features.reshape(cube), order, tiles, w_rel, w_root, upstream.reshape(cube))

    sums, own_sums = pl.pallas_call(
        lambda *refs: push_kernel(groups, *refs),
        grid=(blocks,),
        out_shape=(shape((SPAN * blocks, width, bl), BF), shape((blocks, width, bl), F32)),
        in_specs=[
            smem,
            pl.BlockSpec((1,) + tiles.shape[1:], lambda i: (i, 0, 0, 0)),
            pl.BlockSpec((1, width, bl), lambda i: (i, 0, 0)),
        ],
        out_specs=(
            pl.BlockSpec((SPAN * blocks, width, bl), lambda i: (0, 0, 0)),
            pl.BlockSpec((blocks, width, bl), lambda i: (0, 0, 0)),
        ),
        scratch_shapes=[pltpu.VMEM((SPAN * blocks, width, bl), F32)],
        compiler_params=pltpu.CompilerParams(vmem_limit_bytes=48 * MIB),
        name="push",
    )(columns, tiles, back_agg)

    piece = (2 * width // rows, width)
    grad_feat, grad_rel, grad_root = pl.pallas_call(
        lambda *refs: backward_kernel(groups, *refs),
        out_shape=(
            shape(cube, BF),
            shape((4 * width, width), F32),
            shape((4 * width, width), F32),
        ),
        in_specs=[vmem] * 5,
        out_specs=(vmem,) * 3,
        scratch_shapes=[
            pltpu.VMEM((6 * blocks, width, bl), BF),
            pltpu.VMEM((3 * blocks, width, bl), BF),
            pltpu.VMEM((4, 2 * width, width), BF),
            pltpu.VMEM((4, 2 * width, width), BF),
            pltpu.VMEM((3, 2 * width, width), BF),
            pltpu.VMEM((rows,) + piece, F32),
            pltpu.VMEM((rows,) + piece, F32),
            pltpu.VMEM((4, rows) + piece, F32),
            pltpu.VMEM((rows,) + piece, F32),
            pltpu.VMEM(piece, F32),
            dma((6, BACK_CHUNKS)),
            dma((6, BACK_CHUNKS)),
            dma((3,)), dma((3,)),
            dma((3,)), dma((3,)),
            dma((rows,)), dma((rows,)),
            dma((rows,)), dma((rows,)),
            dma((3,)), dma((3,)),
        ],
        compiler_params=pltpu.CompilerParams(
            collective_id=1, has_side_effects=True, vmem_limit_bytes=48 * MIB
        ),
        name="backward",
    )(sums, own_sums, back_root, order, wgrad)

    flat = (blocks * bl, width)
    return hidden.reshape(flat), grad_feat.reshape(flat), grad_rel, grad_root


def solution(mesh):
    in_specs = (
        P("blk", "rep"),
        P("blk", None),
        P("blk", None),
        P("blk", None, None, None),
        P(None, "rep"),
        P(None, "rep"),
        P("blk", "rep"),
    )
    out_specs = (P("blk", "rep"), P("blk", "rep"), P(None, "rep"), P(None, "rep"))
    return jax.shard_map(
        on_device, mesh=mesh, in_specs=in_specs, out_specs=out_specs, check_vma=False
    )
```

time: 1050 us -> 150 us (0.14)
  waiting for transfers between devices: 816 us -> 0 us
  Pallas kernels: 0 us -> 143 us
  other arithmetic: 63.8 us -> 0 us
  local copies, waits for them, and re-layouts: 66 us -> 5.95 us
  starting transfers between devices: 37 us -> 0 us
  matrix products: 32.3 us -> 0 us
  blocking collectives: 14.8 us -> 0 us
  between operations: 15.4 us -> 0.72 us
    psum x1 -> x0, waiting for transfers between devices: 672 us -> none  [on_device(): lax.psum((jnp.dot(agg_full.T, grad_pre, preferred_element_type=jnp.float3...]
    pallas_call x0 -> x3, Pallas kernels: none -> 143 us  [the longest x1 74.6 us: on_device(): pl.pallas_call(lambda *refs: forward_kernel(groups, *refs), out_shape=(sh...]
    all_gather x3 -> x0, waiting for transfers between devices: 80.2 us -> none  [the longest x1 32.6 us: on_device(): lax.all_gather(ordered_rows, 'rep', axis=1, tiled=True)]
    ppermute x12 -> x0, waiting for transfers between devices: 62.6 us -> none  [passed_along(): return lax.ppermute(value, axis, pairs)]
    scatter-add x1 -> x0, other arithmetic: 52.2 us -> none  [on_device(): jax.ops.segment_sum(contrib.reshape(blocks * per_row, block_len, panel_wi...]
    ppermute x12 -> x0, starting transfers between devices: 36.6 us -> none  [passed_along(): return lax.ppermute(value, axis, pairs)]
    gather x3 -> x0, local copies, waits for them, and re-layouts: 32.9 us -> none  [the longest x1 11.1 us: on_device(): jnp.take_along_axis(grad_ordered, inverse[:, :, None], axis=1)]
    dot_general x8 -> x0, matrix products: 32.3 us -> none  [the longest x1 11.5 us: on_device(): jnp.einsum('bkji,fbj->bkif', tiles, grad_agg, preferred_element_type=jnp....]
  transfers between devices with their start and end apart: 16 -> 0, of which waited for: 12 -> 0; matrix products, arithmetic and copies ran while one was open for 3% -> 0% of each run, Pallas kernels for 0% -> 0%
where the time goes in v1:
time: 150 us
  Pallas kernels  143 us (95%)
  local copies, waits for them, and re-layouts  5.95 us (4%)
    pallas_call x1, Pallas kernels, on_device(): pl.pallas_call(lambda *refs: forward_kernel(groups, *refs), out_shape=(sh...  74.6 us
    pallas_call x1, Pallas kernels, on_device(): pl.pallas_call(lambda *refs: backward_kernel(groups, *refs), out_shape=(s...  55.3 us
    pallas_call x1, Pallas kernels, on_device(): pl.pallas_call(lambda *refs: push_kernel(groups, *refs), grid=(blocks,),...  13.2 us
    unnamed x18, local copies, waits for them, and re-layouts  5.95 us

profile of v1, /device:TPU:2, one launch (start us, length us, event | category | flops | bytes accessed | tf_op | source)
XLA Modules:
  0.0 149.7 jit_solution(12871187450880529459)
XLA Ops:
  0.6 0.0 copy-start.4
  0.6 0.0 copy-start.5
  0.7 74.6 %forward.1 = (bf16[16,128,128]{2,1,0:T(8,128)(2,1)}, bf16[16,128,128]{2,1,0:T(8,128)(2,1)}, f32[16,128,128]{2,1,0:T(8,128)}, f32[4,256,128]{2,1,0:T(8,128)}) custom-call(s32[16,16]{1,0:T(8,128)} %refs_0_.3, bf16[16,128,128]{2,1,0:T(8,128)(2,1)} %bitcast.5, s32[16,128]{1,0:T(8,128)} %refs_3_.3, bf16[16,16,128,128]{3,2,1,0:T(8,128)(2,1)} %refs_1_.1, ...), custom_call_target="tpu_custom_call" | custom-call | tf_op jit(solution)/shard_map/forward/pallas_call | solution.py:505
  75.2 0.0 copy-start.1
  75.2 0.0 copy-start.2
  75.3 0.0 copy-done.4
  75.3 0.0 copy-start.3
  75.3 1.1 copy-done.3
  76.4 0.0 copy-start.6
  76.4 13.2 %push.1 = (bf16[112,128,128]{2,1,0:T(8,128)(2,1)S(1)}, f32[16,128,128]{2,1,0:T(8,128)S(1)}) custom-call(s32[16,16]{1,0:T(8,128)S(1)} %copy-done.4, bf16[16,16,128,128]{3,2,1,0:T(8,128)(2,1)} %refs_1_.1, bf16[16,128,128]{2,1,0:T(8,128)(2,1)S(1)} %copy-done.3), custom_call_target="tpu_custom_call" | custom-call | tf_op jit(solution)/shard_map/push/pallas_call | solution.py:540
  89.6 0.0 copy-start
  89.6 1.8 %copy-done = bf16[112,128,128]{2,1,0:T(8,128)(2,1)} copy-done((bf16[112,128,128]{2,1,0:T(8,128)(2,1)}, bf16[112,128,128]{2,1,0:T(8,128)(2,1)S(1)}, u32[]{:S(2)}) %copy-start) | copy-done | bytes 3670040
  91.4 0.0 copy-done.5
  91.4 0.0 copy-done.1
  91.4 0.0 copy-done.2
  91.4 55.3 %backward.1 = (bf16[16,128,128]{2,1,0:T(8,128)(2,1)S(1)}, f32[512,128]{1,0:T(8,128)S(1)}, f32[512,128]{1,0:T(8,128)S(1)}) custom-call(bf16[112,128,128]{2,1,0:T(8,128)(2,1)} %copy-done, f32[16,128,128]{2,1,0:T(8,128)S(1)} %get-tuple-element.16.refs_1_, f32[16,128,128]{2,1,0:T(8,128)S(1)} %copy-done.1, s32[16,128]{1,0:T(8,128)S(1)} %copy-done.5, ...), custom_call_target="tpu_custom_call" | custom-call | tf_op jit(solution)/shard_map/backward/pallas_call | solution.py:559
  146.7 0.0 copy-done.6
  146.7 0.8 copy.15
  147.5 0.8 copy.16
  148.3 0.7 copy.17
  149.0 0.7 copy.18
Async XLA Ops:
  0.6 74.6 %copy-start.4 = (s32[16,16]{1,0:T(8,128)S(1)}, s32[16,16]{1,0:T(8,128)}, u32[]{:S(2)}) copy-start(s32[16,16]{1,0:T(8,128)} %refs_0_.3) | copy-start | bytes 3076
  0.6 90.8 %copy-start.5 = (s32[16,128]{1,0:T(8,128)S(1)}, s32[16,128]{1,0:T(8,128)}, u32[]{:S(2)}) copy-start(s32[16,128]{1,0:T(8,128)} %refs_3_.3) | copy-start | bytes 24580
  75.2 16.2 %copy-start.1 = (f32[16,128,128]{2,1,0:T(8,128)S(1)}, f32[16,128,128]{2,1,0:T(8,128)}, u32[]{:S(2)}) copy-start(f32[16,128,128]{2,1,0:T(8,128)} %get-tuple-element.17.refs_2_) | copy-start | bytes 3145732
  75.2 16.2 %copy-start.2 = (f32[4,256,128]{2,1,0:T(8,128)S(1)}, f32[4,256,128]{2,1,0:T(8,128)}, u32[]{:S(2)}) copy-start(f32[4,256,128]{2,1,0:T(8,128)} %get-tuple-element.18.refs_4_) | copy-start | bytes 1572868
  75.3 1.2 copy-start.3
  76.4 70.3 %copy-start.6 = (bf16[16,128,128]{2,1,0:T(8,128)(2,1)S(1)}, bf16[16,128,128]{2,1,0:T(8,128)(2,1)}, u32[]{:S(2)}) copy-start(bf16[16,128,128]{2,1,0:T(8,128)(2,1)} %get-tuple-element.13) | copy-start | bytes 1572868
  89.6 1.8 %copy-start = (bf16[112,128,128]{2,1,0:T(8,128)(2,1)}, bf16[112,128,128]{2,1,0:T(8,128)(2,1)S(1)}, u32[]{:S(2)}) copy-start(bf16[112,128,128]{2,1,0:T(8,128)(2,1)S(1)} %get-tuple-element.15.refs_0_) | copy-start | bytes 11010052

commit v2 on v1

v2 whole, which is shorter than its diff:
```python
import jax
import jax.numpy as jnp
from jax import lax
from jax.experimental import pallas as pl
from jax.experimental.pallas import tpu as pltpu
from jax.sharding import PartitionSpec as P

MESH = pl.DeviceIdType.MESH
REACH = 3
SPAN = 2 * REACH + 1
ROW = 4
HALO_CHUNKS = 8
MID_CHUNKS = 8
BACK_CHUNKS = 8
BF = jnp.bfloat16
F32 = jnp.float32
NT = (((1,), (1,)), ((), ()))
TN = (((0,), (0,)), ((), ()))
MIB = 2**20


class Place:
    def __init__(self, groups):
        blk = lax.axis_index("blk")
        rep = lax.axis_index("rep")
        self.groups = groups
        self.rows = groups // ROW
        self.blk, self.rep = blk, rep
        x = lax.rem(blk, ROW)
        self.x = x
        self.row = lax.div(blk, ROW)
        half, odd = lax.div(x, 2), lax.rem(x, 2)
        self.n1 = 3 - x
        self.n2 = x + 1 - 2 * odd
        self.diag = lax.rem(x + 2, 4)
        self.step_p = 1 - 2 * half
        self.step_q = 1 - 2 * odd
        self.slot_n1 = REACH + self.n1 - x
        self.slot_n2 = REACH + self.n2 - x
        self.slot_diag = REACH + self.diag - x
        self.slot_p = REACH + self.n1 - x - ROW * self.step_p
        self.slot_q = REACH + self.n2 - x - ROW * self.step_q
        self.slot_post = 1 + 4 * half
        self.core = lax.rem(rep, 2)
        self.low = lax.div(rep, 2)
        self.rep_sib = 2 * self.low + 1 - self.core
        self.rep_y = 2 * (1 - self.low) + self.core
        self.rep_far = 2 * (1 - self.low) + 1 - self.core

    def at_x(self, x):
        return (self.row * ROW + x, self.rep)

    def at_row(self, row):
        return (row * ROW + self.x, self.rep)

    def row_by(self, step):
        return self.at_row(lax.rem(self.row + step + self.rows, self.rows))

    def near(self, d):
        at = lax.rem(self.x * 4 + self.rep + d, 16)
        return (self.row * ROW + lax.div(at, 4), lax.rem(at, 4))

    def at_rep(self, rep):
        return (self.blk, rep)


def greet(partners):
    barrier = pltpu.get_barrier_semaphore()
    for who in partners:
        pl.semaphore_signal(barrier, inc=1, device_id=who, device_id_type=MESH)
    pl.semaphore_wait(barrier, len(partners))


def remote(src, dst, send, recv, who):
    return pltpu.make_async_remote_copy(
        src_ref=src, dst_ref=dst, send_sem=send, recv_sem=recv, device_id=who, device_id_type=MESH
    )


def onehot(order_ref, b):
    length = order_ref.shape[1]
    node = lax.broadcasted_iota(jnp.int32, (length, length), 0)
    return (node == order_ref[pl.ds(b, 1), :]).astype(F32).astype(BF)


def slot_of(col, place, blocks):
    group = lax.shift_right_arithmetic(col, jnp.int32(blocks.bit_length() - 1))
    offset = (group - place.blk + REACH + place.groups) & (place.groups - 1)
    return jnp.minimum(offset, SPAN - 1) * blocks + (col & (blocks - 1))


def sort_entries(cols_row, place, blocks, meta):
    count = cols_row.shape[1]
    slot = slot_of(cols_row, place, blocks)
    entry = lax.broadcasted_iota(jnp.int32, (count, count), 1)
    slots = jnp.broadcast_to(slot, (count, count))
    slots_t = slots.T
    keys, keys_t = slots * count + entry, slots_t * count + entry.T
    earlier = (keys_t < keys).astype(jnp.int32)
    rank = jnp.sum(earlier, axis=0, keepdims=True)
    same = jnp.sum(jnp.where(slots_t == slots, earlier, 0), axis=0, keepdims=True)
    rank_t = jnp.broadcast_to(rank, (count, count)).T
    same_t = jnp.broadcast_to(same, (count, count)).T
    here = rank_t == entry
    meta[0:1, :] = jnp.sum(jnp.where(here, entry.T, 0), axis=0, keepdims=True)
    meta[1:2, :] = jnp.sum(jnp.where(here, jnp.minimum(same_t, 1), 0), axis=0, keepdims=True)
    upto = jnp.sum((slots_t <= entry).astype(jnp.int32), axis=0, keepdims=True)
    meta[2:3, :] = jnp.maximum(upto - 1, 0)
    found = jnp.sum((slots_t == entry).astype(jnp.int32), axis=0, keepdims=True)
    meta[3:4, :] = jnp.minimum(found, 1)


def layer_kernel(
    groups,
    cols, feat, order, tiles, w_rel, w_root, upstream,
    hidden, grad_feat, grad_rel, grad_root,
    win, tbuf, agg, slab, keep, s1, r1, s2, r2, pre, back_root, wgrad, prod, meta, meta_s,
    land, wsend, a1, a2, a3, a4, piece, done,
    tile_sem, meta_sem, hs, hr, ws, wr, ms, mr,
    bs, br, e0s, e0r, e2s, e2r, e3s, e3r, e4s, e4r,
):
    me = Place(groups)
    blocks, bl, width = feat.shape
    per_row = cols.shape[1]
    entries = blocks * per_row
    own = REACH * blocks
    nc = HALO_CHUNKS
    hb = blocks // nc
    nm = MID_CHUNKS
    mb = blocks // nm
    mrows = mb * bl

    tile_copy = pltpu.make_async_copy(tiles, tbuf, tile_sem)
    tile_copy.start()
    sib, far_y = me.at_rep(me.rep_sib), me.at_rep(me.rep_y)
    greet([me.near(d) for d in range(1, 16)] + [me.row_by(d) for d in range(1, me.rows)])

    def halo(kind, c):
        src_slot, dst_slot, who = [
            (REACH, REACH + me.x - me.n1, me.at_x(me.n1)),
            (REACH, REACH + me.x - me.n2, me.at_x(me.n2)),
            (me.slot_n2, REACH + me.n2 - me.n1, me.at_x(me.n1)),
            (me.slot_n1, me.slot_p, me.row_by(me.step_p)),
            (me.slot_n2, me.slot_q, me.row_by(me.step_q)),
            (me.slot_p, me.slot_post, me.at_x(me.n2)),
        ][kind]
        return remote(
            win.at[pl.ds(src_slot * blocks + c * hb, hb)],
            win.at[pl.ds(dst_slot * blocks + c * hb, hb)],
            hs.at[kind, c], hr.at[kind, c], who,
        )

    @pl.loop(0, nc)
    def _(c):
        for i in range(hb):
            b = c * hb + i
            win[own + b] = lax.dot_general(
                onehot(order, b), feat[b], TN, preferred_element_type=F32
            ).astype(BF)
        halo(0, c).start()
        halo(1, c).start()

    def weight(i, j):
        who = (me.rep_sib, me.rep_y, me.rep_far)[i]
        src = (w_rel, w_root)[j]
        return remote(
            src.at[pl.ds(who * width, width)], slab.at[me.rep, pl.ds(j * width, width)],
            ws.at[i, j], wr.at[i, j], me.at_rep(who),
        )

    for i in range(3):
        for j in range(2):
            weight(i, j).start()
    for j, src in enumerate((w_rel, w_root)):
        slab[me.rep, j * width : (j + 1) * width] = src[pl.ds(me.rep * width, width), :]

    place_of = lax.broadcasted_iota(jnp.int32, (1, entries), 1)

    def collect(b, row):
        for k in range(per_row):
            row = jnp.where(place_of == b * per_row + k, cols[b, k], row)
        return row

    cols_row = lax.fori_loop(0, blocks, collect, jnp.zeros((1, entries), jnp.int32))
    sort_entries(cols_row, me, blocks, meta)
    meta_copy = pltpu.make_async_copy(meta, meta_s, meta_sem)
    meta_copy.start()

    @pl.loop(0, nc + 2)
    def _(s):
        @pl.when(s < nc)
        def _():
            halo(0, s).wait_recv()
            halo(1, s).wait_recv()
            halo(2, s).start()
            halo(3, s).start()
            halo(4, s).start()

        @pl.when(s >= 2)
        def _():
            halo(3, s - 2).wait_recv()
            halo(5, s - 2).start()

    @pl.loop(0, nc)
    def _(c):
        for kind in (2, 4, 5):
            halo(kind, c).wait_recv()

    for i in range(3):
        for j in range(2):
            weight(i, j).wait_recv()
    tile_copy.wait()
    meta_copy.wait()

    panel_sib = [2 * (1 - me.low) + 1 - me.core, 2 * me.low + 1 - me.core]
    panel_mine = [me.rep_y, me.rep]

    def rows(c):
        return pl.ds(c * mb, mb)

    def mid(kind, c):
        src, dst, who = [
            (s1.at[c], r1.at[c], sib),
            (s2.at[c], r2.at[c], far_y),
            (pre.at[me.rep, rows(c)], pre.at[me.rep, rows(c)], far_y),
            (pre.at[me.rep, rows(c)], pre.at[me.rep, rows(c)], sib),
            (pre.at[me.rep_y, rows(c)], pre.at[me.rep_y, rows(c)], sib),
        ][kind]
        return remote(src, dst, ms.at[kind, c], mr.at[kind, c], who)

    def both(c):
        return jnp.concatenate(
            [
                agg[rows(c)].reshape(mrows, width),
                win[pl.ds(own + c * mb, mb)].reshape(mrows, width),
            ],
            axis=1,
        )

    @pl.loop(0, nm + 4)
    def _(s):
        @pl.when(s < nm)
        def _():
            for i in range(mb):
                b = s * mb + i
                left = jnp.concatenate([tbuf[b, k] for k in range(per_row)], axis=1)
                right = jnp.concatenate(
                    [win[slot_of(cols[b, k], me, blocks)] for k in range(per_row)], axis=0
                )
                agg[b] = jnp.dot(left, right, preferred_element_type=F32).astype(BF)
            x = both(s)
            for i in range(2):
                part = jnp.dot(x, slab[panel_sib[i]], preferred_element_type=F32)
                s1[s, i] = part.astype(BF)
            mid(0, s).start()
            for i in range(2):
                keep[s, i] = jnp.dot(x, slab[panel_mine[i]], preferred_element_type=F32)

        @pl.when((s >= 1) & (s < nm + 1))
        def _():
            c = s - 1
            mid(0, c).wait_recv()
            s2[c] = (keep[c, 0] + r1[c, 0].astype(F32)).astype(BF)
            mid(1, c).start()

        @pl.when((s >= 2) & (s < nm + 2))
        def _():
            c = s - 2
            mid(1, c).wait_recv()
            v = keep[c, 1] + r1[c, 1].astype(F32) + r2[c].astype(F32)
            sq = v * v
            t = jnp.tanh(0.7978845608 * (v + 0.044715 * (sq * v)))
            up = upstream[rows(c)].reshape(mrows, width).astype(F32)
            hidden[rows(c)] = (0.5 * v * (1.0 + t)).astype(BF).reshape(mb, bl, width)
            slope = 0.5 * (1.0 + t) + 0.5 * v * (1.0 - t * t) * (
                0.7978845608 * (1.0 + 0.134145 * sq)
            )
            pre[me.rep, rows(c)] = (up * slope).astype(BF).reshape(mb, bl, width)
            mid(2, c).start()
            mid(3, c).start()

        @pl.when((s >= 3) & (s < nm + 3))
        def _():
            mid(2, s - 3).wait_recv()
            mid(4, s - 3).start()

        @pl.when(s >= 4)
        def _():
            c = s - 4
            mid(3, c).wait_recv()
            mid(4, c).wait_recv()
            x = both(c)
            gathered = jnp.concatenate(
                [pre[p, rows(c)].reshape(mrows, width) for p in range(4)], axis=1
            )
            slabs = jnp.concatenate([slab[p] for p in range(4)], axis=1)
            back = lax.dot_general(slabs, gathered, NT, preferred_element_type=F32)
            for i in range(mb):
                cut = back[:, i * bl : (i + 1) * bl]
                b = c * mb + i
                back_root[b] = cut[width:]
                right = jnp.concatenate([tbuf[b, k] for k in range(per_row)], axis=1)
                res = jnp.dot(cut[:width].astype(BF), right, preferred_element_type=F32)
                for k in range(per_row):
                    prod[b * per_row + k] = res[:, k * bl : (k + 1) * bl]
            grads = lax.dot_general(x, gathered, TN, preferred_element_type=F32)

            @pl.when(c == 0)
            def _():
                for p in range(4):
                    wgrad[p] = grads[:, p * width : (p + 1) * width]

            @pl.when(c > 0)
            def _():
                for p in range(4):
                    wgrad[p] += grads[:, p * width : (p + 1) * width]

    na = BACK_CHUNKS
    ab = blocks // na
    rows_all = me.rows
    x_others = [me.n1, me.n2, me.diag]
    POST, DIAG, Q, PP, N2, N1 = range(6)

    def part(ref, slot, c):
        return ref.at[pl.ds(slot * blocks + c * ab, ab)]

    out = win
    @pl.loop(0, nc)
    def _(c):
        for kind in range(6):
            halo(kind, c).wait_send()

    def back(kind, c):
        _, who = [
            (POST, me.at_x(me.n2)),
            (DIAG, me.at_x(me.n1)),
            (Q, me.row_by(-me.step_q)),
            (PP, me.row_by(-me.step_p)),
            (N2, me.at_x(me.n2)),
            (N1, me.at_x(me.n1)),
        ][kind]
        return remote(part(out, kind, c), part(land, kind, c), bs.at[kind, c], br.at[kind, c], who)

    def got(kind, b):
        return land[kind * blocks + b].astype(F32)

    def local(slot, b):
        at = slot * blocks + b
        last = meta_s[2, at]
        return tbuf[lax.div(last, per_row), lax.rem(last, per_row)].astype(F32) * meta_s[3, at].astype(F32)

    alone = me.x == me.rep

    def give(p):
        return remote(
            wsend.at[p], a1.at[me.x], e0s.at[p], e0r.at[me.x], (me.row * ROW + me.rep, p)
        )

    def take(x):
        return remote(wsend.at[0], a1.at[x], e0s.at[0], e0r.at[x], (me.row * ROW + x, me.x))

    def unless_self(i, mine, act):
        @pl.when(jnp.logical_not(alone & (mine == i)))
        def _():
            act(i)

    def scatter_rows(d):
        who = lax.rem(me.row + d, rows_all)
        return remote(piece.at[who], a2.at[d], e2s.at[d], e2r.at[d], me.at_row(who))

    def gather_rows(d):
        who = lax.rem(me.row + d, rows_all)
        return remote(done, a3.at[me.row], e3s.at[d], e3r.at[d], me.at_row(who))

    def gather_x(i):
        return remote(a3, a4.at[me.x], e4s.at[i], e4r.at[i], me.at_x(x_others[i]))

    for p in range(4):
        wsend[p] = wgrad[p].astype(BF)
    for p in range(4):
        unless_self(p, me.rep, lambda i: give(i).start())

    @pl.when(alone)
    def _():
        a1[me.x] = wsend[me.rep]

    def add(e, total):
        total = total * meta_s[1, e].astype(F32) + prod[meta_s[0, e]]
        tbuf[lax.div(e, per_row), lax.rem(e, per_row)] = total.astype(BF)
        return total

    lax.fori_loop(0, entries, add, jnp.zeros((width, bl), F32), unroll=4)
    for x in range(4):
        unless_self(x, me.x, lambda i: take(i).wait_recv())
    summed = a1[0].astype(F32)
    for x in range(1, 4):
        summed += a1[x].astype(F32)
    piece[...] = summed.reshape(piece.shape)
    for d in range(1, rows_all):
        scatter_rows(d).start()

    @pl.loop(0, na + 6)
    def _(s):
        @pl.when(s < na)
        def _():
            c = s
            for kind, slot in ((POST, me.slot_post), (DIAG, me.slot_diag), (Q, me.slot_q)):
                for i in range(ab):
                    b = c * ab + i
                    out[kind * blocks + b] = local(slot, b).astype(BF)
                back(kind, c).start()

        @pl.when((s >= 2) & (s < na + 2))
        def _():
            c = s - 2
            back(POST, c).wait_recv()
            for i in range(ab):
                b = c * ab + i
                out[PP * blocks + b] = (local(me.slot_p, b) + got(POST, b)).astype(BF)
            back(PP, c).start()

        @pl.when((s >= 4) & (s < na + 4))
        def _():
            c = s - 4
            back(DIAG, c).wait_recv()
            back(Q, c).wait_recv()
            for i in range(ab):
                b = c * ab + i
                out[N2 * blocks + b] = (local(me.slot_n2, b) + got(DIAG, b) + got(Q, b)).astype(BF)
            back(N2, c).start()

        @pl.when((s >= 4) & (s < na + 4))
        def _():
            c = s - 4
            back(PP, c).wait_recv()
            for i in range(ab):
                b = c * ab + i
                out[N1 * blocks + b] = (local(me.slot_n1, b) + got(PP, b)).astype(BF)
            back(N1, c).start()

        @pl.when(s == 3)
        def _():
            for d in range(1, rows_all):
                scatter_rows(d).wait_recv()
            total = piece[me.row]
            for d in range(1, rows_all):
                total += a2[d]
            done[...] = total.astype(BF)
            a3[me.row] = total.astype(BF)
            for d in range(1, rows_all):
                gather_rows(d).start()

        @pl.when(s == 7)
        def _():
            for d in range(1, rows_all):
                gather_rows(d).wait_recv()
            for i in range(3):
                gather_x(i).start()
            a4[me.x] = a3[...]

        @pl.when(s >= 6)
        def _():
            c = s - 6
            back(N2, c).wait_recv()
            back(N1, c).wait_recv()
            for i in range(ab):
                b = c * ab + i
                total = local(REACH, b) + back_root[b] + got(N1, b) + got(N2, b)
                grad_feat[b] = lax.dot_general(
                    onehot(order, b), total.astype(BF), NT, preferred_element_type=F32
                ).astype(BF)

    for i in range(3):
        gather_x(i).wait_recv()
    for p in range(4):
        both = a4[p].reshape(2 * width, width).astype(F32)
        grad_rel[p * width : (p + 1) * width, :] = both[:width]
        grad_root[p * width : (p + 1) * width, :] = both[width:]

    @pl.loop(0, na)
    def _(c):
        for kind in range(6):
            back(kind, c).wait_send()

    for i in range(3):
        gather_x(i).wait_send()
    for p in range(4):
        unless_self(p, me.rep, lambda i: give(i).wait_send())
    for d in range(1, rows_all):
        scatter_rows(d).wait_send()
        gather_rows(d).wait_send()

    @pl.loop(0, nm)
    def _(c):
        for kind in range(5):
            mid(kind, c).wait_send()

    for i in range(3):
        for j in range(2):
            weight(i, j).wait_send()


def on_device(features, order, columns, tiles, w_rel, w_root, upstream):
    groups = lax.axis_size("blk")
    blocks, bl = order.shape
    width = features.shape[1]
    rows = groups // ROW
    vmem = pl.BlockSpec(memory_space=pltpu.VMEM)
    smem = pl.BlockSpec(memory_space=pltpu.SMEM)
    anywhere = pl.BlockSpec(memory_space=pl.ANY)
    dma = pltpu.SemaphoreType.DMA
    cube = (blocks, bl, width)
    mrows = blocks // MID_CHUNKS * bl

    def shape(dims, dtype):
        return jax.ShapeDtypeStruct(dims, dtype)

    piece = (2 * width // rows, width)
    entries = columns.size
    hidden, grad_feat, grad_rel, grad_root = pl.pallas_call(
        lambda *refs: layer_kernel(groups, *refs),
        out_shape=(
            shape(cube, BF),
            shape(cube, BF),
            shape((4 * width, width), F32),
            shape((4 * width, width), F32),
        ),
        in_specs=[smem, vmem, vmem, anywhere, vmem, vmem, vmem],
        out_specs=(vmem,) * 4,
        scratch_shapes=[
            pltpu.VMEM((SPAN * blocks, bl, width), BF),
            pltpu.VMEM(tiles.shape, BF),
            pltpu.VMEM(cube, BF),
            pltpu.VMEM((4, 2 * width, width), BF),
            pltpu.VMEM((MID_CHUNKS, 2, mrows, width), F32),
            pltpu.VMEM((MID_CHUNKS, 2, mrows, width), BF),
            pltpu.VMEM((MID_CHUNKS, 2, mrows, width), BF),
            pltpu.VMEM((MID_CHUNKS, mrows, width), BF),
            pltpu.VMEM((MID_CHUNKS, mrows, width), BF),
            pltpu.VMEM((4,) + cube, BF),
            pltpu.VMEM((blocks, width, bl), F32),
            pltpu.VMEM((4, 2 * width, width), F32),
            pltpu.VMEM((entries, width, bl), F32),
            pltpu.VMEM((8, entries), jnp.int32),
            pltpu.SMEM((8, entries), jnp.int32),
            pltpu.VMEM((6 * blocks, width, bl), BF),
            pltpu.VMEM((4, 2 * width, width), BF),
            pltpu.VMEM((4, 2 * width, width), BF),
            pltpu.VMEM((rows,) + piece, F32),
            pltpu.VMEM((rows,) + piece, BF),
            pltpu.VMEM((4, rows) + piece, BF),
            pltpu.VMEM((rows,) + piece, F32),
            pltpu.VMEM(piece, BF),
            dma(()),
            dma(()),
            dma((6, HALO_CHUNKS)),
            dma((6, HALO_CHUNKS)),
            dma((3, 2)),
            dma((3, 2)),
            dma((5, MID_CHUNKS)),
            dma((5, MID_CHUNKS)),
            dma((6, BACK_CHUNKS)),
            dma((6, BACK_CHUNKS)),
            dma((4,)), dma((4,)),
            dma((rows,)), dma((rows,)),
            dma((rows,)), dma((rows,)),
            dma((3,)), dma((3,)),
        ],
        compiler_params=pltpu.CompilerParams(
            collective_id=0, has_side_effects=True, vmem_limit_bytes=46 * MIB
        ),
        name="layer",
    )(
        columns, features.reshape(cube), order, tiles, w_rel, w_root,
        upstream.reshape(cube),
    )

    flat = (blocks * bl, width)
    return hidden.reshape(flat), grad_feat.reshape(flat), grad_rel, grad_root


def solution(mesh):
    in_specs = (
        P("blk", "rep"),
        P("blk", None),
        P("blk", None),
        P("blk", None, None, None),
        P(None, "rep"),
        P(None, "rep"),
        P("blk", "rep"),
    )
    out_specs = (P("blk", "rep"), P("blk", "rep"), P(None, "rep"), P(None, "rep"))
    return jax.shard_map(
        on_device, mesh=mesh, in_specs=in_specs, out_specs=out_specs, check_vma=False
    )
```

time: 150 us -> 134 us (0.89)
  the two profiles are of different devices: /device:TPU:2 before, /device:TPU:10 now
where the time goes in v2:
time: 134 us
  Pallas kernels  125 us (93%)
  local copies, waits for them, and re-layouts  8.27 us (6%)
    pallas_call x1, Pallas kernels, on_device(): pl.pallas_call(lambda *refs: layer_kernel(groups, *refs), out_shape=(shap...  125 us
    unnamed x16, local copies, waits for them, and re-layouts  8.27 us

profile of v2, /device:TPU:10, one launch (start us, length us, event | category | flops | bytes accessed | tf_op | source)
XLA Modules:
  0.0 133.7 jit_solution(16007774360249269758)
XLA Ops:
  0.6 0.0 copy-start
  0.6 1.0 copy-done
  1.7 0.0 copy-start.1
  1.7 1.0 copy-done.1
  2.7 0.0 copy-start.2
  2.7 0.9 copy-done.2
  3.6 0.0 copy-start.3
  3.6 0.9 copy-done.3
  4.5 0.0 copy-start.4
  4.5 0.7 copy-done.4
  5.2 0.0 copy-start.5
  5.2 0.7 copy-done.5
  5.9 124.8 %layer.1 = (bf16[16,128,128]{2,1,0:T(8,128)(2,1)S(1)}, bf16[16,128,128]{2,1,0:T(8,128)(2,1)S(1)}, f32[512,128]{1,0:T(8,128)S(1)}, f32[512,128]{1,0:T(8,128)S(1)}) custom-call(s32[16,16]{1,0:T(8,128)S(1)} %copy-done.4, bf16[16,128,128]{2,1,0:T(8,128)(2,1)S(1)} %bitcast.4, s32[16,128]{1,0:T(8,128)S(1)} %copy-done.5, bf16[16,16,128,128]{3,2,1,0:T(8,128)(2,1)} %refs_3_.1, ...), custom_call_target="tpu_custom_call" | custom-call | tf_op jit(solution)/shard_map/layer/pallas_call | solution.py:520
  130.8 0.8 copy.15
  131.5 0.8 copy.16
  132.3 0.7 copy.17
  133.0 0.7 copy.18
Async XLA Ops:
  0.6 1.0 copy-start
  1.7 1.0 copy-start.1
  2.7 0.9 copy-start.2
  3.6 0.9 copy-start.3
  4.5 0.7 copy-start.4
  5.2 0.7 copy-start.5

commit v3 on v2

--- a/solution.py
+++ b/solution.py
@@ -9,9 +9,12 @@
 REACH = 3
 SPAN = 2 * REACH + 1
 ROW = 4
-HALO_CHUNKS = 8
+HALO_CHUNKS = 4
 MID_CHUNKS = 8
-BACK_CHUNKS = 8
+BACK_CHUNKS = 16
+MID_LAGS = (1, 3, 5, 6)
+BACK_LAGS = (2, 5, 8)
+WGRAD_STEPS = (5, 11, 17)
 BF = jnp.bfloat16
 F32 = jnp.float32
 NT = (((1,), (1,)), ((), ()))
@@ -112,11 +115,11 @@
 
 def layer_kernel(
     groups,
-    cols, feat, order, tiles, w_rel, w_root, upstream,
+    cols_in, feat_in, order_in, tiles, w_rel_in, w_root_in, upstream_in,
     hidden, grad_feat, grad_rel, grad_root,
-    win, tbuf, agg, slab, keep, s1, r1, s2, r2, pre, back_root, wgrad, prod, meta, meta_s,
+    cols, feat, order, w_rel, w_root, upstream, win, tbuf, agg, slab, keep, s1, r1, s2, r2, pre, back_root, wgrad, prod, meta, meta_s,
     land, wsend, a1, a2, a3, a4, piece, done,
-    tile_sem, meta_sem, hs, hr, ws, wr, ms, mr,
+    in_sem, tile_sem, meta_sem, hs, hr, ws, wr, ms, mr,
     bs, br, e0s, e0r, e2s, e2r, e3s, e3r, e4s, e4r,
 ):
     me = Place(groups)
@@ -130,10 +133,28 @@
     mb = blocks // nm
     mrows = mb * bl
 
+    loads = [
+        pltpu.make_async_copy(src, dst, in_sem.at[i])
+        for i, (src, dst) in enumerate(
+            (
+                (feat_in, feat),
+                (order_in, order),
+                (w_rel_in, w_rel),
+                (w_root_in, w_root),
+                (cols_in, cols),
+                (upstream_in, upstream),
+            )
+        )
+    ]
+    for load in loads:
+        load.start()
     tile_copy = pltpu.make_async_copy(tiles, tbuf, tile_sem)
     tile_copy.start()
     sib, far_y = me.at_rep(me.rep_sib), me.at_rep(me.rep_y)
     greet([me.near(d) for d in range(1, 16)] + [me.row_by(d) for d in range(1, me.rows)])
+
+    loads[0].wait()
+    loads[1].wait()
 
     def halo(kind, c):
         src_slot, dst_slot, who = [
@@ -160,6 +181,9 @@
         halo(0, c).start()
         halo(1, c).start()
 
+    for load in loads[2:5]:
+        load.wait()
+
     def weight(i, j):
         who = (me.rep_sib, me.rep_y, me.rep_far)[i]
         src = (w_rel, w_root)[j]
@@ -210,6 +234,7 @@
         for j in range(2):
             weight(i, j).wait_recv()
     tile_copy.wait()
+    loads[5].wait()
     meta_copy.wait()
 
     panel_sib = [2 * (1 - me.low) + 1 - me.core, 2 * me.low + 1 - me.core]
@@ -237,7 +262,9 @@
             axis=1,
         )
 
-    @pl.loop(0, nm + 4)
+    lag_b, lag_c, lag_d, lag_e = MID_LAGS
+
+    @pl.loop(0, nm + lag_e)
     def _(s):
         @pl.when(s < nm)
         def _():
@@ -256,16 +283,16 @@
             for i in range(2):
                 keep[s, i] = jnp.dot(x, slab[panel_mine[i]], preferred_element_type=F32)
 
-        @pl.when((s >= 1) & (s < nm + 1))
-        def _():
-            c = s - 1
+        @pl.when((s >= lag_b) & (s < nm + lag_b))
+        def _():
+            c = s - lag_b
             mid(0, c).wait_recv()
             s2[c] = (keep[c, 0] + r1[c, 0].astype(F32)).astype(BF)
             mid(1, c).start()
 
-        @pl.when((s >= 2) & (s < nm + 2))
-        def _():
-            c = s - 2
+        @pl.when((s >= lag_c) & (s < nm + lag_c))
+        def _():
+            c = s - lag_c
             mid(1, c).wait_recv()
             v = keep[c, 1] + r1[c, 1].astype(F32) + r2[c].astype(F32)
             sq = v * v
@@ -279,14 +306,14 @@
             mid(2, c).start()
             mid(3, c).start()
 
-        @pl.when((s >= 3) & (s < nm + 3))
-        def _():
-            mid(2, s - 3).wait_recv()
-            mid(4, s - 3).start()
-
-        @pl.when(s >= 4)
-        def _():
-            c = s - 4
+        @pl.when((s >= lag_d) & (s < nm + lag_d))
+        def _():
+            mid(2, s - lag_d).wait_recv()
+            mid(4, s - lag_d).start()
+
+        @pl.when(s >= lag_e)
+        def _():
+            c = s - lag_e
             mid(3, c).wait_recv()
             mid(4, c).wait_recv()
             x = both(c)
@@ -389,17 +416,10 @@
         tbuf[lax.div(e, per_row), lax.rem(e, per_row)] = total.astype(BF)
         return total
 
-    lax.fori_loop(0, entries, add, jnp.zeros((width, bl), F32), unroll=4)
-    for x in range(4):
-        unless_self(x, me.x, lambda i: take(i).wait_recv())
-    summed = a1[0].astype(F32)
-    for x in range(1, 4):
-        summed += a1[x].astype(F32)
-    piece[...] = summed.reshape(piece.shape)
-    for d in range(1, rows_all):
-        scatter_rows(d).start()
-
-    @pl.loop(0, na + 6)
+    lax.fori_loop(0, entries, add, jnp.zeros((width, bl), F32), unroll=8)
+    lag_p, lag_n, lag_out = BACK_LAGS
+
+    @pl.loop(0, na + lag_out)
     def _(s):
         @pl.when(s < na)
         def _():
@@ -410,18 +430,18 @@
                     out[kind * blocks + b] = local(slot, b).astype(BF)
                 back(kind, c).start()
 
-        @pl.when((s >= 2) & (s < na + 2))
-        def _():
-            c = s - 2
+        @pl.when((s >= lag_p) & (s < na + lag_p))
+        def _():
+            c = s - lag_p
             back(POST, c).wait_recv()
             for i in range(ab):
                 b = c * ab + i
                 out[PP * blocks + b] = (local(me.slot_p, b) + got(POST, b)).astype(BF)
             back(PP, c).start()
 
-        @pl.when((s >= 4) & (s < na + 4))
-        def _():
-            c = s - 4
+        @pl.when((s >= lag_n) & (s < na + lag_n))
+        def _():
+            c = s - lag_n
             back(DIAG, c).wait_recv()
             back(Q, c).wait_recv()
             for i in range(ab):
@@ -429,16 +449,27 @@
                 out[N2 * blocks + b] = (local(me.slot_n2, b) + got(DIAG, b) + got(Q, b)).astype(BF)
             back(N2, c).start()
 
-        @pl.when((s >= 4) & (s < na + 4))
-        def _():
-            c = s - 4
+        @pl.when((s >= lag_n) & (s < na + lag_n))
+        def _():
+            c = s - lag_n
             back(PP, c).wait_recv()
             for i in range(ab):
                 b = c * ab + i
                 out[N1 * blocks + b] = (local(me.slot_n1, b) + got(PP, b)).astype(BF)
             back(N1, c).start()
 
-        @pl.when(s == 3)
+        @pl.when(s == WGRAD_STEPS[0])
+        def _():
+            for x in range(4):
+                unless_self(x, me.x, lambda i: take(i).wait_recv())
+            summed = a1[0].astype(F32)
+            for x in range(1, 4):
+                summed += a1[x].astype(F32)
+            piece[...] = summed.reshape(piece.shape)
+            for d in range(1, rows_all):
+                scatter_rows(d).start()
+
+        @pl.when(s == WGRAD_STEPS[1])
         def _():
             for d in range(1, rows_all):
                 scatter_rows(d).wait_recv()
@@ -450,7 +481,7 @@
             for d in range(1, rows_all):
                 gather_rows(d).start()
 
-        @pl.when(s == 7)
+        @pl.when(s == WGRAD_STEPS[2])
         def _():
             for d in range(1, rows_all):
                 gather_rows(d).wait_recv()
@@ -458,9 +489,9 @@
                 gather_x(i).start()
             a4[me.x] = a3[...]
 
-        @pl.when(s >= 6)
-        def _():
-            c = s - 6
+        @pl.when(s >= lag_out)
+        def _():
+            c = s - lag_out
             back(N2, c).wait_recv()
             back(N1, c).wait_recv()
             for i in range(ab):
@@ -506,8 +537,7 @@
     width = features.shape[1]
     rows = groups // ROW
     vmem = pl.BlockSpec(memory_space=pltpu.VMEM)
-    smem = pl.BlockSpec(memory_space=pltpu.SMEM)
-    anywhere = pl.BlockSpec(memory_space=pl.ANY)
+    hbm = pl.BlockSpec(memory_space=pltpu.HBM)
     dma = pltpu.SemaphoreType.DMA
     cube = (blocks, bl, width)
     mrows = blocks // MID_CHUNKS * bl
@@ -525,9 +555,15 @@
             shape((4 * width, width), F32),
             shape((4 * width, width), F32),
         ),
-        in_specs=[smem, vmem, vmem, anywhere, vmem, vmem, vmem],
+        in_specs=[hbm] * 7,
         out_specs=(vmem,) * 4,
         scratch_shapes=[
+            pltpu.SMEM(columns.shape, jnp.int32),
+            pltpu.VMEM(cube, BF),
+            pltpu.VMEM(order.shape, jnp.int32),
+            pltpu.VMEM(w_rel.shape, BF),
+            pltpu.VMEM(w_root.shape, BF),
+            pltpu.VMEM(cube, BF),
             pltpu.VMEM((SPAN * blocks, bl, width), BF),
             pltpu.VMEM(tiles.shape, BF),
             pltpu.VMEM(cube, BF),
@@ -551,6 +587,7 @@
             pltpu.VMEM((4, rows) + piece, BF),
             pltpu.VMEM((rows,) + piece, F32),
             pltpu.VMEM(piece, BF),
+            dma((6,)),
             dma(()),
             dma(()),
             dma((6, HALO_CHUNKS)),
@@ -567,7 +604,7 @@
             dma((3,)), dma((3,)),
         ],
         compiler_params=pltpu.CompilerParams(
-            collective_id=0, has_side_effects=True, vmem_limit_bytes=46 * MIB
+            collective_id=0, has_side_effects=True, vmem_limit_bytes=52 * MIB
         ),
         name="layer",
     )(

time: 134 us -> 122 us (0.910)
  the two profiles are of different devices: /device:TPU:10 before, /device:TPU:2 now
where the time goes in v3:
time: 122 us
  Pallas kernels  115 us (94%)
  local copies, waits for them, and re-layouts  6.19 us (5%)
    pallas_call x1, Pallas kernels, on_device(): pl.pallas_call(lambda *refs: layer_kernel(groups, *refs), out_shape=(shap...  115 us
    unnamed x12, local copies, waits for them, and re-layouts  6.19 us

profile of v3, /device:TPU:2, one launch (start us, length us, event | category | flops | bytes accessed | tf_op | source)
XLA Modules:
  0.0 121.6 jit_solution(10311934852676971919)
XLA Ops:
  0.6 0.0 copy-start
  0.6 0.9 copy-done
  1.5 0.0 copy-start.1
  1.5 0.9 copy-done.1
  2.4 0.0 copy-start.2
  2.4 0.7 copy-done.2
  3.1 0.0 copy-start.3
  3.1 0.7 copy-done.3
  3.8 114.8 %layer.1 = (bf16[16,128,128]{2,1,0:T(8,128)(2,1)S(1)}, bf16[16,128,128]{2,1,0:T(8,128)(2,1)S(1)}, f32[512,128]{1,0:T(8,128)S(1)}, f32[512,128]{1,0:T(8,128)S(1)}) custom-call(s32[16,16]{1,0:T(8,128)S(1)} %copy-done.2, bf16[16,128,128]{2,1,0:T(8,128)(2,1)} %bitcast.6, s32[16,128]{1,0:T(8,128)S(1)} %copy-done.3, bf16[16,16,128,128]{3,2,1,0:T(8,128)(2,1)} %refs_3_.1, ...), custom_call_target="tpu_custom_call" | custom-call | tf_op jit(solution)/shard_map/layer/pallas_call | solution.py:550
  118.6 0.8 copy.15
  119.4 0.8 copy.16
  120.2 0.7 copy.17
  120.9 0.7 copy.18
Async XLA Ops:
  0.6 0.9 copy-start
  1.5 0.9 copy-start.1
  2.4 0.7 copy-start.2
  3.1 0.7 copy-start.3

commit v4 on v3

--- a/solution.py
+++ b/solution.py
@@ -216,9 +216,9 @@
         def _():
             halo(0, s).wait_recv()
             halo(1, s).wait_recv()
-            halo(2, s).start()
             halo(3, s).start()
             halo(4, s).start()
+            halo(2, s).start()
 
         @pl.when(s >= 2)
         def _():

time: 122 us -> 122 us (level)
  no operation moved by 1% of the time
where the time goes in v4:
time: 122 us
  Pallas kernels  115 us (94%)
  local copies, waits for them, and re-layouts  6.19 us (5%)
    pallas_call x1, Pallas kernels, on_device(): pl.pallas_call(lambda *refs: layer_kernel(groups, *refs), out_shape=(shap...  115 us
    unnamed x12, local copies, waits for them, and re-layouts  6.19 us

profile of v4, /device:TPU:2, one launch (start us, length us, event | category | flops | bytes accessed | tf_op | source)
XLA Modules:
  0.0 121.6 jit_solution(14631742815219261847)
XLA Ops:
  0.6 0.0 copy-start
  0.6 0.9 copy-done
  1.5 0.0 copy-start.1
  1.5 0.9 copy-done.1
  2.4 0.0 copy-start.2
  2.4 0.7 copy-done.2
  3.1 0.0 copy-start.3
  3.1 0.7 copy-done.3
  3.8 114.8 %layer.1 = (bf16[16,128,128]{2,1,0:T(8,128)(2,1)S(1)}, bf16[16,128,128]{2,1,0:T(8,128)(2,1)S(1)}, f32[512,128]{1,0:T(8,128)S(1)}, f32[512,128]{1,0:T(8,128)S(1)}) custom-call(s32[16,16]{1,0:T(8,128)S(1)} %copy-done.2, bf16[16,128,128]{2,1,0:T(8,128)(2,1)} %bitcast.6, s32[16,128]{1,0:T(8,128)S(1)} %copy-done.3, bf16[16,16,128,128]{3,2,1,0:T(8,128)(2,1)} %refs_3_.1, ...), custom_call_target="tpu_custom_call" | custom-call | tf_op jit(solution)/shard_map/layer/pallas_call | solution.py:550
  118.6 0.8 copy.15
  119.4 0.8 copy.16
  120.2 0.7 copy.17
  120.9 0.7 copy.18
Async XLA Ops:
  0.6 0.9 copy-start
  1.5 0.9 copy-start.1
  2.4 0.7 copy-start.2
  3.1 0.7 copy-start.3
